TPU v7x, 32 devices: a whole 2x2x4 slice. The times are simulated.
32 devices in a mesh: opg: 8 (over z, x), sec: 4 (over y, core).
Axes of the slice: x: 2, y: 2, z: 4, core: 2. Of those that a mesh axis runs over, the one named last changes fastest.
Arguments:
- psi: bfloat16 [8, 384, 384], P('sec'), may hold values from -6 to 6
- left_ops: bfloat16 [64, 8, 384, 384], P('opg', 'sec'), may hold values from -0.15625 to 0.15625
- right_ops: bfloat16 [64, 8, 384, 384], P('opg', 'sec'), may hold values from -0.109375 to 0.109375
- source: int32 [64, 8], P('opg', 'sec'), may hold values from 0 to 7
- coef_index: int32 [64, 8], P('opg', 'sec'), may hold values from 0 to 63
- sixj: float32 [64], replicated, may hold values from -1 to 1
Outputs:
- sigma: bfloat16 [384, 8, 384], P('opg', 'sec')
All inputs are finite; a program needn't handle non-finite values.
Results may differ from a plain program's by a relative error of at most 0.005.
Values may be sent and summed in bfloat16 or wider, within the bound.
No kernel may reach another device: no remote copies, remote signals or barrier semaphores. Data moves between devices by JAX's collectives and lax.ppermute only.
A program may use at most 64 MiB of HBM per device.

v0:
```python
import jax
import jax.numpy as jnp
from jax import lax
from jax.sharding import PartitionSpec as P


def on_device(psi, left_ops, right_ops, source, coef_index, sixj):
    whole = lax.all_gather(psi, "sec", axis=0, tiled=True)
    picked = whole[source]
    table_ids = jnp.arange(sixj.shape[0], dtype=jnp.int32)
    onehot = (coef_index[:, :, None] == table_ids[None, None, :]).astype(jnp.float32)
    coef = jnp.sum(onehot * sixj[None, None, :], axis=-1)
    half = jnp.einsum(
        "psib,psbc->psic", left_ops, picked, preferred_element_type=jnp.float32
    ).astype(jnp.bfloat16)
    full = jnp.einsum("psic,psjc->psij", half, right_ops, preferred_element_type=jnp.float32)
    summed = jnp.sum(full * coef[:, :, None, None], axis=0)
    mine = lax.psum_scatter(
        jnp.transpose(summed, (1, 0, 2)), "opg", scatter_dimension=0, tiled=True
    )
    return mine.astype(jnp.bfloat16)


def solution(mesh):
    placed = (
        P("sec", None, None),
        P("opg", "sec", None, None),
        P("opg", "sec", None, None),
        P("opg", "sec"),
        P("opg", "sec"),
        P(),
    )
    return jax.shard_map(
        on_device, mesh=mesh, in_specs=placed, out_specs=P("opg", "sec", None), check_vma=False
    )
```

profile of v0, /device:TPU:0, one launch (start us, length us, event | category | flops | bytes accessed | tf_op | source)
XLA Modules:
  0.0 132.0 jit_solution(5295882061414146267)
XLA Ops:
  6.5 0.0 all-gather.2.cloned.1.call-start
  6.5 0.7 all-gather.2.cloned.1.call-update
  7.3 0.7 compare_select_fusion
  7.9 0.1 copy.16
  8.0 0.1 reshape.5
  8.1 0.9 select_reduce_fusion
  9.0 0.1 copy.19
  9.1 1.2 dynamic-slice
  11.0 24.8 %all-gather.2.cloned.1.call-done = bf16[8,384,384]{2,1,0:T(8,128)(2,1)} async-done(((bf16[2,384,384]{2,1,0:T(8,128)(2,1)}), bf16[8,384,384]{2,1,0:T(8,128)(2,1)}) %all-gather.2.cloned.1.call-update) | async-done | bytes 2359312 | tf_op jit(solution)/shard_map/all_gather | solution.py:8
  35.7 5.0 %gather_fusion = bf16[16,384,384]{2,1,0:T(8,128)(2,1)} fusion(bf16[8,384,384]{2,1,0:T(8,128)(2,1)} %all-gather.2.cloned.1.call-done, s32[1024]{0:T(1024)S(1)} %pad_clamp_fusion), kind=kCustom, calls=%fused_computation | custom fusion | bytes 9437248 | tf_op jit(solution)/shard_map/gather | solution.py:9
  40.7 9.9 %multiply_reduce_fusion = f32[2,384,384]{2,1,0:T(8,128)S(1)} fusion(f32[8,2]{1,0:T(8,128)S(1)} %copy.19, bf16[8,2,384,384]{3,2,1,0:T(8,128)(2,1)} %param.8, bf16[8,2,384,384]{3,2,1,0:T(8,128)(2,1)} %bitcast.6, bf16[8,2,384,384]{3,2,1,0:T(8,128)(2,1)} %param.7), kind=kOutput, calls=%fused_computation.1 | convolution fusion | flops 3630661632 | bytes 15335488 | tf_op jit(solution)/shard_map/psic,psjc->psij/dot_general | solution.py:16
  50.6 0.9 copy.20
  51.5 72.9 %all-reduce.2 = bf16[384,2,384]{2,1,0:T(2,128)(2,1)S(1)} all-reduce(f32[384,2,384]{2,1,0:T(2,128)S(1)} %copy.20), channel_id=2, replica_groups=mesh['opg'=8,'sec'=4] {'opg'}, use_global_device_ids=true, to_apply=%region_2.0.clone | all-reduce | flops 294912 | bytes 1769472
  124.4 0.7 dynamic-slice_convert_fusion
  (1 shorter events, 0.0 us)
Async XLA Ops:
  6.5 29.2 %all-gather.2.cloned.1.call-start = ((), (), s32[]{:S(2)}) async-start(), calls=%async_computation | async-start | bytes 2949120 | tf_op jit(solution)/shard_map/all_gather | solution.py:8
Sparse Core Ops, SparseCore 0:
  8.9 26.7 all-gather.1
where the time goes:
time: 132 us
  blocking collectives  72.9 us (55%)
  waiting for transfers between devices  25.5 us (19%)
  between operations  14.1 us (11%)
  matrix products  9.88 us (7%)
  local copies, waits for them, and re-layouts  8.09 us (6%)
  other arithmetic  1.54 us (1%)
    unnamed x1, blocking collectives  72.9 us
    all_gather x1, waiting for transfers between devices, on_device(): whole = lax.all_gather(psi, 'sec', axis=0, tiled=True)  24.8 us
    dot_general x1, matrix products, on_device(): jnp.einsum('psic,psjc->psij', half, right_ops, preferred_element_type=jnp...  9.88 us
    gather x1, local copies, waits for them, and re-layouts, on_device(): picked = whole[source]  5 us
  transfers between devices with their start and end apart: 1, of which 1 were waited for; matrix products, arithmetic and copies ran while one was open for 2% of the time, Pallas kernels for 0%

commit v1 on v0

v1 whole, which is shorter than its diff:
```python
import functools

import jax
import jax.numpy as jnp
from jax import lax
from jax.experimental import pallas as pl
from jax.experimental.pallas import tpu as pltpu
from jax.sharding import PartitionSpec as P

OPG = "opg"
SEC = "sec"
PARTS = 4
NEAR = 2
TILE = 256
KERNEL_VMEM = 24_000_000
PLAN_FLOPS = 20_000_000_000


def flip(x, axis, size, bit):
    return lax.ppermute(x, axis, [(i, i ^ bit) for i in range(size)])


def bits_of(size):
    return [1 << k for k in range(size.bit_length() - 1)]


def tiles(size):
    return [slice(at, min(at + TILE, size)) for at in range(0, size, TILE)]


CLASSES = 3


def make_plan(meta, plan, scale, pairs, local):
    slots = local * pairs
    for kind in range(CLASSES):
        plan[kind, 3 * slots] = 0
    me_sec = lax.axis_index(SEC)

    def sector(s):
        def one(p, carry):
            src = meta[s, p].astype(jnp.int32)
            r, j = lax.div(src, local) ^ me_sec, lax.rem(src, local)
            kind = jnp.where(r < NEAR, 0, 1 + lax.rem(r, 2))
            block = jnp.where(r < NEAR, r, lax.div(r, 2) - 1) * local + j
            n = plan[kind, 3 * slots]
            plan[kind, n] = p
            plan[kind, slots + n] = s
            plan[kind, 2 * slots + n] = block
            scale[kind, n] = meta[local + s, p]
            plan[kind, 3 * slots] = n + 1
            return carry

        lax.fori_loop(0, pairs, one, 0)

    for s in range(local):
        sector(s)


def run(kind, plan, scale, left, right, psi, acc, even, odd):
    pairs, local, sb, _ = left.shape
    slots = local * pairs
    count = plan[kind, 3 * slots]

    def first(i, halves):
        i = jnp.minimum(i, count - 1)
        p, s, block = [plan[kind, k * slots + i] for k in range(3)]
        half = jnp.dot(left[p, s], psi[block], preferred_element_type=jnp.float32)
        halves[...] = (half * scale[kind, i]).astype(jnp.bfloat16)

    def second(i, halves):
        p, s = [plan[kind, k * slots + i] for k in range(2)]
        for c in tiles(sb):
            for k in tiles(sb):
                acc[s, :, c] += lax.dot_general(
                    halves[:, k],
                    right[p, s, c, k],
                    (((1,), (1,)), ((), ())),
                    preferred_element_type=jnp.float32,
                )

    def two(j, carry):
        i = 2 * j
        first(i + 1, odd)
        second(i, even)
        first(i + 2, even)
        second(i + 1, odd)
        return carry

    @pl.when(count > 0)
    def _():
        first(0, even)
        lax.fori_loop(0, lax.div(count, 2), two, 0)

        @pl.when(lax.rem(count, 2) == 1)
        def _():
            second(count - 1, even)


def plan_kernel(local, meta, plan, scale):
    make_plan(meta, plan, scale, meta.shape[1], local)


def products_kernel(kind, n_opg, plan, scale, left, right, *refs):
    local, sb = left.shape[1:3]
    last = kind == CLASSES - 1
    outs = n_opg if last else 1
    pieces, refs = refs[: -outs - 3 - last], refs[-outs - 3 - last :]
    psi, even, odd = refs[outs : outs + 3]
    acc = refs[-1] if last else refs[0]
    if kind:
        acc[...] = pieces[0][...]
        pieces = pieces[1:]
    else:
        acc[...] = jnp.zeros_like(acc)
    if len(pieces) == 1:
        psi = pieces[0]
    else:
        for i, piece in enumerate(pieces):
            psi[i * local : (i + 1) * local] = piece[...]
    run(kind, plan, scale, left, right, psi, acc, even, odd)
    if last:
        me_opg = lax.axis_index(OPG)
        rows = sb // n_opg
        for r, send in enumerate(refs[:outs]):
            at = pl.multiple_of((r ^ me_opg) * rows, 8)
            send[...] = acc[:, pl.ds(at, rows), :].astype(send.dtype)


SMEM = pl.BlockSpec(memory_space=pltpu.SMEM)
VMEM = pl.BlockSpec(memory_space=pltpu.VMEM)


def products(kind, n_opg, plan, scale, left, right, totals, pieces):
    pairs, local, sb, _ = left.shape
    out_shape = jax.ShapeDtypeStruct((local, sb, sb), jnp.float32)
    scratch = []
    if kind == CLASSES - 1:
        scratch = [pltpu.VMEM(out_shape.shape, out_shape.dtype)]
        out_shape = tuple(
            jax.ShapeDtypeStruct(
                (local, sb // n_opg, sb), jnp.bfloat16 if r % PARTS else jnp.float32
            )
            for r in range(n_opg)
        )
    return pl.pallas_call(
        functools.partial(products_kernel, kind, n_opg),
        out_shape=out_shape,
        in_specs=[SMEM] * 2 + [VMEM] * (2 + len(totals) + len(pieces)),
        out_specs=jax.tree.map(lambda _: VMEM, out_shape),
        scratch_shapes=[
            pltpu.VMEM((len(pieces) * local, sb, sb), jnp.bfloat16),
            pltpu.VMEM((sb, sb), jnp.bfloat16),
            pltpu.VMEM((sb, sb), jnp.bfloat16),
            *scratch,
        ],
        compiler_params=pltpu.CompilerParams(vmem_limit_bytes=KERNEL_VMEM),
        cost_estimate=pl.CostEstimate(flops=sb, bytes_accessed=0, transcendentals=0),
    )(plan, scale, left, right, *totals, *pieces)


def scatter_sum(sends, n_opg):
    out = []
    for high in reversed(range(n_opg // PARTS)):
        at = high * PARTS
        total = sends[at]
        for low in (3, 1, 2):
            total = total + flip(sends[at + low], OPG, n_opg, low).astype(jnp.float32)
        if high:
            total = flip(total.astype(jnp.bfloat16), OPG, n_opg, at).astype(jnp.float32)
        out.append(total)
    return sum(out[:-1], out[-1])


def on_device(n_opg, n_sec, psi, left_ops, right_ops, source, coef_index, sixj):
    local = psi.shape[0]
    pairs = left_ops.shape[0]

    twins = {0: psi}
    for bit in bits_of(n_sec)[1:]:
        twins.update({r | bit: flip(x, SEC, n_sec, bit) for r, x in twins.items()})
    twins = [twins[r] for r in range(NEAR, n_sec, 2)]
    partner = flip(psi, SEC, n_sec, 1)

    table = jnp.arange(sixj.shape[0], dtype=jnp.int32)
    coef = jnp.sum(jnp.where(coef_index.T[:, :, None] == table, sixj, 0.0), axis=2)
    meta = jnp.concatenate([source.T.astype(jnp.float32), coef])
    plan, scale = pl.pallas_call(
        functools.partial(plan_kernel, local),
        out_shape=(
            jax.ShapeDtypeStruct((CLASSES, 3 * local * pairs + 1), jnp.int32),
            jax.ShapeDtypeStruct((CLASSES, local * pairs), jnp.float32),
        ),
        in_specs=[SMEM],
        out_specs=(SMEM, SMEM),
        compiler_params=pltpu.CompilerParams(vmem_limit_bytes=KERNEL_VMEM),
        cost_estimate=pl.CostEstimate(flops=PLAN_FLOPS, bytes_accessed=0, transcendentals=0),
    )(meta)

    def onto(kind, totals, pieces):
        return products(kind, n_opg, plan, scale, left_ops, right_ops, totals, pieces)

    done = onto(0, [], [psi, partner])
    twins, done = lax.optimization_barrier((twins, done))
    others = [flip(x, SEC, n_sec, 1) for x in twins]
    done = onto(1, [done], twins)
    sends = onto(2, [done], others)
    return jnp.swapaxes(scatter_sum(sends, n_opg), 0, 1).astype(jnp.bfloat16)


def solution(mesh):
    n_opg, n_sec = mesh.shape[OPG], mesh.shape[SEC]
    placed = (
        P(SEC, None, None),
        P(OPG, SEC, None, None),
        P(OPG, SEC, None, None),
        P(OPG, SEC),
        P(OPG, SEC),
        P(),
    )
    return jax.shard_map(
        functools.partial(on_device, n_opg, n_sec),
        mesh=mesh,
        in_specs=placed,
        out_specs=P(OPG, SEC, None),
        check_vma=False,
    )
```

time: 132 us -> 39.2 us (0.30)
  blocking collectives: 72.9 us -> 0 us
  waiting for transfers between devices: 25.5 us -> 9.91 us
  between operations: 14.1 us -> 0.09 us
  Pallas kernels: 0 us -> 12.2 us
  starting transfers between devices: 0.01 us -> 12 us
  matrix products: 9.88 us -> 0 us
  local copies, waits for them, and re-layouts: 8.09 us -> 2.77 us
    unnamed x1 -> x0, blocking collectives: 72.9 us -> none
    all_gather x1 -> x0, waiting for transfers between devices: 24.8 us -> none  [on_device(): whole = lax.all_gather(psi, 'sec', axis=0, tiled=True)]
    pallas_call x0 -> x4, Pallas kernels: none -> 12.2 us  [the longest x3 10.4 us: products(): pl.pallas_call(functools.partial(products_kernel, kind, n_opg), out_shape...]
    ppermute x0 -> x10, starting transfers between devices: none -> 12 us  [flip(): return lax.ppermute(x, axis, [(i, i ^ bit) for i in range(size)])]
    ppermute x0 -> x10, waiting for transfers between devices: none -> 9.91 us  [flip(): return lax.ppermute(x, axis, [(i, i ^ bit) for i in range(size)])]
    dot_general x1 -> x0, matrix products: 9.88 us -> none  [on_device(): jnp.einsum('psic,psjc->psij', half, right_ops, preferred_element_type=jnp...]
    gather x1 -> x0, local copies, waits for them, and re-layouts: 5 us -> none  [on_device(): picked = whole[source]]
  transfers between devices with their start and end apart: 1 -> 10, of which waited for: 1 -> 4; matrix products, arithmetic and copies ran while one was open for 2% -> 4% of each run, Pallas kernels for 0% -> 20%
where the time goes in v1:
time: 39.2 us; the launch traced here: 38.6 us
  Pallas kernels  12.2 us (31%)
  starting transfers between devices  12 us (31%)
  waiting for transfers between devices  9.91 us (25%)
  local copies, waits for them, and re-layouts  2.77 us (7%)
  other arithmetic  1.64 us (4%)
    ppermute x10, starting transfers between devices, flip(): return lax.ppermute(x, axis, [(i, i ^ bit) for i in range(size)])  12 us
    pallas_call x3, Pallas kernels, products(): pl.pallas_call(functools.partial(products_kernel, kind, n_opg), out_shape...  10.4 us
    ppermute x10, waiting for transfers between devices, flip(): return lax.ppermute(x, axis, [(i, i ^ bit) for i in range(size)])  9.91 us
    unnamed x6, local copies, waits for them, and re-layouts  2.08 us
    pallas_call x1, Pallas kernels, on_device(): pl.pallas_call(functools.partial(plan_kernel, local), out_shape=(jax.Shap...  1.71 us
    reduce_sum x1, other arithmetic, on_device(): jnp.sum(jnp.where(coef_index.T[:, :, None] == table, sixj, 0.0), axis=2)  0.85 us
  transfers between devices with their start and end apart: 10, of which 4 were waited for; matrix products, arithmetic and copies ran while one was open for 4% of the time, Pallas kernels for 20%

profile of v1, /device:TPU:0, one launch (start us, length us, event | category | flops | bytes accessed | tf_op | source)
XLA Modules:
  0.0 38.6 jit_solution(2691955668013625483)
XLA Ops:
  0.0 3.0 %collective-permute-start = (bf16[2,384,384]{2,1,0:T(8,128)(2,1)}, bf16[2,384,384]{2,1,0:T(8,128)(2,1)S(1)}, u32[]{:S(2)}, u32[]{:S(2)}) collective-permute-start(bf16[2,384,384]{2,1,0:T(8,128)(2,1)} %refs_0_.1), channel_id=1, source_target_pairs={{0,2},{1,3},{2,0},{3,1},{4,6},{5,7},{6,4},{7,5},{8,10},{9,11},{10,... | collective-permute-start | bytes 1769480 | tf_op jit(solution)/shard_map/ppermute | solution.py:20
  3.0 0.0 collective-permute-start.1
  3.0 0.7 %convert_bitcast_fusion = f32[2,8]{1,0:T(2,128)S(1)} fusion(s32[8,2]{0,1:T(2,128)} %param.9), kind=kLoop, calls=%fused_computation.6 | loop fusion | flops 16 | bytes 128 | tf_op jit(solution)/shard_map/convert_element_type | solution.py:187
  3.7 0.8 %select_reduce_fusion = f32[2,8]{1,0:T(2,128)S(1)} fusion(f32[64]{0:T(128)} %param.11, s32[2,8]{1,0:T(2,128)} %bitcast.5), kind=kLoop, calls=%fused_computation.3 | loop fusion | flops 3056 | bytes 384 | tf_op jit(solution)/shard_map/reduce_sum | solution.py:186
  4.5 0.0 copy-start.1
  4.5 0.0 copy-start.2
  4.5 1.7 %shard_map.64 = (s32[3,49]{1,0:T(4,128)S(1)}, f32[3,16]{1,0:T(4,128)S(1)}) custom-call(f32[4,8]{1,0:T(4,128)S(1)} %pad_maximum_fusion.meta), custom_call_target="tpu_custom_call" | custom-call | flops 20000000000 | tf_op jit(solution)/shard_map/pallas_call | solution.py:188
  6.3 0.0 collective-permute-done.1.refs_1_
  6.3 0.6 %copy-done = bf16[8,2,384,384]{3,2,1,0:T(8,128)(2,1)S(1)} copy-done((bf16[8,2,384,384]{3,2,1,0:T(8,128)(2,1)S(1)}, bf16[8,2,384,384]{3,2,1,0:T(8,128)(2,1)}, u32[]{:S(2)}) %copy-start) | copy-done | bytes 4718616
  6.9 1.4 %copy-done.1 = bf16[8,2,384,384]{3,2,1,0:T(8,128)(2,1)S(1)} copy-done((bf16[8,2,384,384]{3,2,1,0:T(8,128)(2,1)S(1)}, bf16[8,2,384,384]{3,2,1,0:T(8,128)(2,1)}, u32[]{:S(2)}) %copy-start.1) | copy-done | bytes 4718616
  8.3 0.0 copy-done.2
  8.3 2.4 %shard_map.65.refs_0_ = f32[2,384,384]{2,1,0:T(8,128)S(1)} custom-call(s32[3,49]{1,0:T(4,128)S(1)} %get-tuple-element.17.plan, f32[3,16]{1,0:T(4,128)S(1)} %get-tuple-element.18.scale, bf16[8,2,384,384]{3,2,1,0:T(8,128)(2,1)S(1)} %copy-done, bf16[8,2,384,384]{3,2,1,0:T(8,128)(2,1)S(1)} %copy-done.1, bf16[2,384,384]{2,1,0:T(8,128)(2,1)S(1)} %copy-done.2, ...), custom_call_target="tpu_custom_call" | custom-call | flops 384 | tf_op jit(solution)/shard_map/pallas_call | solution.py:146
  10.7 5.8 %collective-permute-done.refs_1_ = bf16[2,384,384]{2,1,0:T(8,128)(2,1)S(1)} collective-permute-done((bf16[2,384,384]{2,1,0:T(8,128)(2,1)}, bf16[2,384,384]{2,1,0:T(8,128)(2,1)S(1)}, u32[]{:S(2)}, u32[]{:S(2)}) %collective-permute-start) | collective-permute-done | bytes 589856 | tf_op jit(solution)/shard_map/ppermute | solution.py:20
  16.5 0.0 collective-permute-start.2
  16.5 3.8 %shard_map.66.refs_0_ = f32[2,384,384]{2,1,0:T(8,128)S(1)} custom-call(s32[3,49]{1,0:T(4,128)S(1)} %get-tuple-element.17.plan, f32[3,16]{1,0:T(4,128)S(1)} %get-tuple-element.18.scale, bf16[8,2,384,384]{3,2,1,0:T(8,128)(2,1)S(1)} %copy-done, bf16[8,2,384,384]{3,2,1,0:T(8,128)(2,1)S(1)} %copy-done.1, f32[2,384,384]{2,1,0:T(8,128)S(1)} %shard_map.65.refs_0_, ...), custom_call_target="tpu_custom_call" | custom-call | flops 384 | tf_op jit(solution)/shard_map/pallas_call | solution.py:146
  20.3 0.0 collective-permute-done.2.refs_1_
  20.3 4.3 %shard_map.67 = (f32[2,48,384]{2,1,0:T(8,128)S(1)}, bf16[2,48,384]{2,1,0:T(8,128)(2,1)S(1)}, bf16[2,48,384]{2,1,0:T(8,128)(2,1)S(1)}, bf16[2,48,384]{2,1,0:T(8,1...) custom-call(s32[3,49]{1,0:T(4,128)S(1)} %get-tuple-element.17.plan, ...), custom_call_target="tpu_custom_call" | custom-call | flops 384 | tf_op jit(solution)/shard_map/pallas_call | solution.py:146
  24.6 0.9 %collective-permute-start.6 = (bf16[2,48,384]{2,1,0:T(8,128)(2,1)S(1)}, bf16[2,48,384]{2,1,0:T(8,128)(2,1)S(1)}, u32[]{:S(2)}, u32[]{:S(2)}) collective-permute-start(bf16[2,48,384]{2,1,0:T(8,128)(2,1)S(1)} %get-tuple-element.26), channel_id=1, source_target_pairs={{0,12},{4,8},{8,4},{12,0},{16,28},{20,24},{24,20},{28,16},{1,13},{... | collective-permute-start | bytes 221192 | tf_op jit(solution)/shard_map/ppermute | solution.py:20
  25.5 2.6 %collective-permute-start.8 = (bf16[2,48,384]{2,1,0:T(8,128)(2,1)S(1)}, bf16[2,48,384]{2,1,0:T(8,128)(2,1)S(1)}, u32[]{:S(2)}, u32[]{:S(2)}) collective-permute-start(bf16[2,48,384]{2,1,0:T(8,128)(2,1)S(1)} %get-tuple-element.28), channel_id=1, source_target_pairs={{0,8},{4,12},{8,0},{12,4},{16,24},{20,28},{24,16},{28,20},{1,9},{5... | collective-permute-start | bytes 221192 | tf_op jit(solution)/shard_map/ppermute | solution.py:20
  28.1 0.9 %collective-permute-start.3 = (bf16[2,48,384]{2,1,0:T(8,128)(2,1)S(1)}, bf16[2,48,384]{2,1,0:T(8,128)(2,1)S(1)}, u32[]{:S(2)}, u32[]{:S(2)}) collective-permute-start(bf16[2,48,384]{2,1,0:T(8,128)(2,1)S(1)} %get-tuple-element.22), channel_id=1, source_target_pairs={{0,12},{4,8},{8,4},{12,0},{16,28},{20,24},{24,20},{28,16},{1,13},{... | collective-permute-start | bytes 221192 | tf_op jit(solution)/shard_map/ppermute | solution.py:20
  29.0 0.6 %collective-permute-start.4 = (bf16[2,48,384]{2,1,0:T(8,128)(2,1)S(1)}, bf16[2,48,384]{2,1,0:T(8,128)(2,1)S(1)}, u32[]{:S(2)}, u32[]{:S(2)}) collective-permute-start(bf16[2,48,384]{2,1,0:T(8,128)(2,1)S(1)} %get-tuple-element.23), channel_id=1, source_target_pairs={{0,4},{4,0},{8,12},{12,8},{16,20},{20,16},{24,28},{28,24},{1,5},{5... | collective-permute-start | bytes 221192 | tf_op jit(solution)/shard_map/ppermute | solution.py:20
  29.6 0.8 %collective-permute-done.6 = bf16[2,48,384]{2,1,0:T(8,128)(2,1)S(1)} collective-permute-done((bf16[2,48,384]{2,1,0:T(8,128)(2,1)S(1)}, bf16[2,48,384]{2,1,0:T(8,128)(2,1)S(1)}, u32[]{:S(2)}, u32[]{:S(2)}) %collective-permute-start.6) | collective-permute-done | bytes 73760 | tf_op jit(solution)/shard_map/ppermute | solution.py:20
  30.4 1.3 %collective-permute-start.5 = (bf16[2,48,384]{2,1,0:T(8,128)(2,1)S(1)}, bf16[2,48,384]{2,1,0:T(8,128)(2,1)S(1)}, u32[]{:S(2)}, u32[]{:S(2)}) collective-permute-start(bf16[2,48,384]{2,1,0:T(8,128)(2,1)S(1)} %get-tuple-element.24), channel_id=1, source_target_pairs={{0,8},{4,12},{8,0},{12,4},{16,24},{20,28},{24,16},{28,20},{1,9},{5... | collective-permute-start | bytes 221192 | tf_op jit(solution)/shard_map/ppermute | solution.py:20
  31.6 0.0 collective-permute-done.7
  31.6 0.0 collective-permute-done.8
  31.7 2.7 %collective-permute-start.9 = (bf16[2,48,384]{2,1,0:T(8,128)(2,1)S(1)}, bf16[2,48,384]{2,1,0:T(8,128)(2,1)S(1)}, u32[]{:S(2)}, u32[]{:S(2)}) collective-permute-start(bf16[2,48,384]{2,1,0:T(8,128)(2,1)S(1)} %add_convert_fusion.1), channel_id=1, source_target_pairs={{0,16},{4,20},{8,24},{12,28},{16,0},{20,4},{24,8},{28,12},{1,17},{... | collective-permute-start | bytes 221192 | tf_op jit(solution)/shard_map/ppermute | solution.py:20
  34.4 0.0 collective-permute-done.3
  34.4 0.0 collective-permute-done.4
  34.4 0.3 collective-permute-done.5
  34.8 3.0 %collective-permute-done.9 = bf16[2,48,384]{2,1,0:T(8,128)(2,1)S(1)} collective-permute-done((bf16[2,48,384]{2,1,0:T(8,128)(2,1)S(1)}, bf16[2,48,384]{2,1,0:T(8,128)(2,1)S(1)}, u32[]{:S(2)}, u32[]{:S(2)}) %collective-permute-start.9) | collective-permute-done | bytes 73760 | tf_op jit(solution)/shard_map/ppermute | solution.py:20
  37.8 0.1 fusion
  37.9 0.7 %copy.8 = bf16[48,2,384]{2,1,0:T(2,128)(2,1)} copy(bf16[48,2,384]{2,0,1:T(8,128)(2,1)S(1)} %fusion) | data formatting | bytes 147456 | tf_op jit(solution)/shard_map/convert_element_type | solution.py:208
  (4 shorter events, 0.1 us)
Async XLA Ops:
  0.0 16.5 %collective-permute-start = (bf16[2,384,384]{2,1,0:T(8,128)(2,1)}, bf16[2,384,384]{2,1,0:T(8,128)(2,1)S(1)}, u32[]{:S(2)}, u32[]{:S(2)}) collective-permute-start(bf16[2,384,384]{2,1,0:T(8,128)(2,1)} %refs_0_.1), channel_id=1, source_target_pairs={{0,2},{1,3},{2,0},{3,1},{4,6},{5,7},{6,4},{7,5},{8,10},{9,11},{10,... | collective-permute-start | bytes 1769480 | tf_op jit(solution)/shard_map/ppermute | solution.py:20
  3.0 3.3 %collective-permute-start.1 = (bf16[2,384,384]{2,1,0:T(8,128)(2,1)}, bf16[2,384,384]{2,1,0:T(8,128)(2,1)S(1)}, u32[]{:S(2)}, u32[]{:S(2)}) collective-permute-start(bf16[2,384,384]{2,1,0:T(8,128)(2,1)} %refs_0_.1), channel_id=1, source_target_pairs={{0,1},{1,0},{2,3},{3,2},{4,5},{5,4},{6,7},{7,6},{8,9},{9,8},{10,11... | collective-permute-start | bytes 1769480 | tf_op jit(solution)/shard_map/ppermute | solution.py:20
  4.5 2.3 %copy-start = (bf16[8,2,384,384]{3,2,1,0:T(8,128)(2,1)S(1)}, bf16[8,2,384,384]{3,2,1,0:T(8,128)(2,1)}, u32[]{:S(2)}) copy-start(bf16[8,2,384,384]{3,2,1,0:T(8,128)(2,1)} %left.5) | copy-start | bytes 14155780
  4.5 3.8 %copy-start.1 = (bf16[8,2,384,384]{3,2,1,0:T(8,128)(2,1)S(1)}, bf16[8,2,384,384]{3,2,1,0:T(8,128)(2,1)}, u32[]{:S(2)}) copy-start(bf16[8,2,384,384]{3,2,1,0:T(8,128)(2,1)} %right.5) | copy-start | bytes 14155780
  4.5 3.8 %copy-start.2 = (bf16[2,384,384]{2,1,0:T(8,128)(2,1)S(1)}, bf16[2,384,384]{2,1,0:T(8,128)(2,1)}, u32[]{:S(2)}) copy-start(bf16[2,384,384]{2,1,0:T(8,128)(2,1)} %refs_0_.1) | copy-start | bytes 1769476
  16.5 3.8 %collective-permute-start.2 = (bf16[2,384,384]{2,1,0:T(8,128)(2,1)S(1)}, bf16[2,384,384]{2,1,0:T(8,128)(2,1)S(1)}, u32[]{:S(2)}, u32[]{:S(2)}) collective-permute-start(bf16[2,384,384]{2,1,0:T(8,128)(2,1)S(1)} %collective-permute-done.refs_1_), channel_id=1, source_target_pairs={{0,1},{1,0},{2,3},{3,2},{4,5},{5,4},{6,7},{7,6},{8,9},{9,8},{10,11... | collective-permute-start | bytes 1769480 | tf_op jit(solution)/shard_map/ppermute | solution.py:20
  24.6 5.8 %collective-permute-start.6 = (bf16[2,48,384]{2,1,0:T(8,128)(2,1)S(1)}, bf16[2,48,384]{2,1,0:T(8,128)(2,1)S(1)}, u32[]{:S(2)}, u32[]{:S(2)}) collective-permute-start(bf16[2,48,384]{2,1,0:T(8,128)(2,1)S(1)} %get-tuple-element.26), channel_id=1, source_target_pairs={{0,12},{4,8},{8,4},{12,0},{16,28},{20,24},{24,20},{28,16},{1,13},{... | collective-permute-start | bytes 221192 | tf_op jit(solution)/shard_map/ppermute | solution.py:20
  25.5 6.1 %collective-permute-start.7 = (bf16[2,48,384]{2,1,0:T(8,128)(2,1)S(1)}, bf16[2,48,384]{2,1,0:T(8,128)(2,1)S(1)}, u32[]{:S(2)}, u32[]{:S(2)}) collective-permute-start(bf16[2,48,384]{2,1,0:T(8,128)(2,1)S(1)} %get-tuple-element.27), channel_id=1, source_target_pairs={{0,4},{4,0},{8,12},{12,8},{16,20},{20,16},{24,28},{28,24},{1,5},{5... | collective-permute-start | bytes 221192 | tf_op jit(solution)/shard_map/ppermute | solution.py:20
  25.5 6.1 %collective-permute-start.8 = (bf16[2,48,384]{2,1,0:T(8,128)(2,1)S(1)}, bf16[2,48,384]{2,1,0:T(8,128)(2,1)S(1)}, u32[]{:S(2)}, u32[]{:S(2)}) collective-permute-start(bf16[2,48,384]{2,1,0:T(8,128)(2,1)S(1)} %get-tuple-element.28), channel_id=1, source_target_pairs={{0,8},{4,12},{8,0},{12,4},{16,24},{20,28},{24,16},{28,20},{1,9},{5... | collective-permute-start | bytes 221192 | tf_op jit(solution)/shard_map/ppermute | solution.py:20
  28.1 6.3 %collective-permute-start.3 = (bf16[2,48,384]{2,1,0:T(8,128)(2,1)S(1)}, bf16[2,48,384]{2,1,0:T(8,128)(2,1)S(1)}, u32[]{:S(2)}, u32[]{:S(2)}) collective-permute-start(bf16[2,48,384]{2,1,0:T(8,128)(2,1)S(1)} %get-tuple-element.22), channel_id=1, source_target_pairs={{0,12},{4,8},{8,4},{12,0},{16,28},{20,24},{24,20},{28,16},{1,13},{... | collective-permute-start | bytes 221192 | tf_op jit(solution)/shard_map/ppermute | solution.py:20
  29.0 5.4 %collective-permute-start.4 = (bf16[2,48,384]{2,1,0:T(8,128)(2,1)S(1)}, bf16[2,48,384]{2,1,0:T(8,128)(2,1)S(1)}, u32[]{:S(2)}, u32[]{:S(2)}) collective-permute-start(bf16[2,48,384]{2,1,0:T(8,128)(2,1)S(1)} %get-tuple-element.23), channel_id=1, source_target_pairs={{0,4},{4,0},{8,12},{12,8},{16,20},{20,16},{24,28},{28,24},{1,5},{5... | collective-permute-start | bytes 221192 | tf_op jit(solution)/shard_map/ppermute | solution.py:20
  30.4 4.4 %collective-permute-start.5 = (bf16[2,48,384]{2,1,0:T(8,128)(2,1)S(1)}, bf16[2,48,384]{2,1,0:T(8,128)(2,1)S(1)}, u32[]{:S(2)}, u32[]{:S(2)}) collective-permute-start(bf16[2,48,384]{2,1,0:T(8,128)(2,1)S(1)} %get-tuple-element.24), channel_id=1, source_target_pairs={{0,8},{4,12},{8,0},{12,4},{16,24},{20,28},{24,16},{28,20},{1,9},{5... | collective-permute-start | bytes 221192 | tf_op jit(solution)/shard_map/ppermute | solution.py:20
  31.7 6.1 %collective-permute-start.9 = (bf16[2,48,384]{2,1,0:T(8,128)(2,1)S(1)}, bf16[2,48,384]{2,1,0:T(8,128)(2,1)S(1)}, u32[]{:S(2)}, u32[]{:S(2)}) collective-permute-start(bf16[2,48,384]{2,1,0:T(8,128)(2,1)S(1)} %add_convert_fusion.1), channel_id=1, source_target_pairs={{0,16},{4,20},{8,24},{12,28},{16,0},{20,4},{24,8},{28,12},{1,17},{... | collective-permute-start | bytes 221192 | tf_op jit(solution)/shard_map/ppermute | solution.py:20
